TPU v7x, 32 devices: a whole 2x2x4 slice. The times are simulated.
32 devices in a mesh: parts: 2 (over x), tensor: 8 (over z, y), section: 2 (over core).
Axes of the slice: x: 2, y: 2, z: 4, core: 2. Of those that a mesh axis runs over, the one named last changes fastest.
Arguments:
- tokens: bfloat16 [2048, 8192], P(('parts', 'section'), 'tensor'), parts along dimension 0
- decode_hidden_rows: bfloat16 [2048, 8192], P(('parts', 'section'), 'tensor'), parts along dimension 0
- query_matrix: bfloat16 [8192, 8192], P(None, 'tensor'), may hold values from -0.0625 to 0.0625
- key_value_matrix: bfloat16 [8192, 2048], P(None, 'tensor'), may hold values from -0.0625 to 0.0625
- adapter_slot_pool: bfloat16 [16, 8192, 128], P('tensor'), may hold values from -0.0625 to 0.0625
- adapter_slot_map: int32 [16], replicated, may hold values from 0 to 15, each once
- tenant_adapter_index: int32 [16], P(('parts', 'section')), parts along dimension 0, may hold values from 0 to 15
- decode_page_table: int32 [2048, 32], P(('parts', 'section')), parts along dimension 0, may hold values from 0 to 63, as said below
- lengths: int32 [2048], P(('parts', 'section')), parts along dimension 0, may hold values from 1 to 512, as said below
Outputs:
- prefill_heads: bfloat16 [2048, 8192], P(('parts', 'section'), 'tensor'), parts along dimension 0
- decode_heads: bfloat16 [2048, 8192], P(('parts', 'section'), 'tensor'), parts along dimension 0
There are 2 independent parts, one for each index of `parts`. A program takes and returns all parts, laid end to end along the dimension named above; an argument that names none is the same for every part. Nothing has to cross between parts.
Inputs may be any that keep to these rules, and one draw needn't show every extreme that they name: `adapter_slot_map`: each slot 0 to 15 once; slot s lies on index s // 2 of tensor. `decode_page_table`: the 32 pages of a row are distinct. `lengths`: some row has the full length.
All inputs are finite; a program needn't handle non-finite values.
Results may differ from a plain program's by a relative error of at most 0.0045.
The roundings to bfloat16 on the way count: a program that leaves them out, or rounds other values in their place, can miss the bound.
Values may be sent and summed in bfloat16 or wider, within the bound.
A program may use at most 192 MiB of HBM per device.

v0:
```python
import math

import jax
import jax.numpy as jnp
from jax import lax
from jax.sharding import PartitionSpec as P

HQ = 64
KVH = 8
HD = 128
ADAPTER_RANK = 64
CTOK = 128
POOL_PER_INDEX = 2
PAGE = 16
PPR = 32


ADAPTER_SCALE = 2.0


def broadcast(block, axis, source):
    block = jnp.where(lax.axis_index(axis) == source, block, jnp.zeros_like(block))
    return lax.psum(block, axis)


def softmax_with_own(scores, live, own_score):
    masked = jnp.where(live, scores, -jnp.inf)
    top = jnp.maximum(jnp.max(masked, axis=-1), own_score)
    dec_exp = jnp.exp(masked - top[..., None])
    own_exp = jnp.exp(own_score - top)
    total = jnp.sum(dec_exp, axis=-1) + own_exp
    return (
        (dec_exp / total[..., None]).astype(jnp.bfloat16),
        (own_exp / total).astype(jnp.bfloat16),
    )


def on_device(
    tokens,
    decode_hidden_rows,
    query_matrix,
    key_value_matrix,
    adapter_slot_pool,
    adapter_slot_map,
    tenant_adapter_index,
    decode_page_table,
    lengths,
):
    scale = 1.0 / math.sqrt(HD)
    group = HQ // KVH
    token_rows_local = tokens.shape[0]
    row_here = decode_hidden_rows.shape[0]
    feature_cols = tokens.shape[1]
    head_cols = query_matrix.shape[1]
    heads_here = head_cols // HD
    stretch_count = token_rows_local // CTOK
    device_index = lax.axis_index("tensor")
    pieces = []
    for c in range(stretch_count):
        pool_slot = adapter_slot_map[tenant_adapter_index[c]]
        local_unit = lax.dynamic_index_in_dim(
            adapter_slot_pool, pool_slot % POOL_PER_INDEX, 0, keepdims=False
        )
        whole = broadcast(local_unit, "tensor", pool_slot // POOL_PER_INDEX)
        pieces.append(lax.dynamic_slice_in_dim(whole, device_index * feature_cols, feature_cols, 0))
    picked = jnp.stack(pieces)
    blocks = tokens.reshape(stretch_count, CTOK, feature_cols)
    low_part = jnp.einsum(
        "ctd,cdr->ctr", blocks, picked[:, :, :ADAPTER_RANK], preferred_element_type=jnp.float32
    )
    low_rank = lax.psum(low_part, "tensor").astype(jnp.bfloat16)
    adapter_update = jnp.einsum(
        "ctr,cdr->ctd", low_rank, picked[:, :, ADAPTER_RANK:], preferred_element_type=jnp.float32
    )
    adapter_update = adapter_update.reshape(token_rows_local, head_cols)
    rows_all = jnp.concatenate(
        (
            lax.all_gather(tokens, "tensor", axis=1, tiled=True),
            lax.all_gather(decode_hidden_rows, "tensor", axis=1, tiled=True),
        ),
        axis=0,
    )
    query_total_sum = jnp.dot(rows_all, query_matrix, preferred_element_type=jnp.float32)
    keyval_sum = jnp.dot(rows_all, key_value_matrix, preferred_element_type=jnp.float32)
    query_token_rows = (query_total_sum[:token_rows_local] + ADAPTER_SCALE * adapter_update).astype(
        jnp.bfloat16
    )
    query_dec = query_total_sum[token_rows_local:].astype(jnp.bfloat16)
    keyval_mine = keyval_sum.astype(jnp.bfloat16)
    key_cols = KVH * HD
    kv_here = max(1, heads_here // group)
    keyval_all = lax.all_gather(keyval_mine, "tensor", axis=1, tiled=True)
    kv_first = device_index * heads_here // group
    keys_mine = lax.dynamic_slice_in_dim(keyval_all, kv_first * HD, kv_here * HD, 1)
    vals_mine = lax.dynamic_slice_in_dim(keyval_all, key_cols + kv_first * HD, kv_here * HD, 1)
    causal = jnp.arange(CTOK)[:, None] >= jnp.arange(CTOK)[None, :]
    prefill_parts = []
    for i in range(heads_here):
        which = i // group
        query_h = query_token_rows[:, i * HD : (i + 1) * HD].reshape(stretch_count, CTOK, HD)
        keys_h = keys_mine[:token_rows_local, which * HD : (which + 1) * HD].reshape(
            stretch_count, CTOK, HD
        )
        vals_h = vals_mine[:token_rows_local, which * HD : (which + 1) * HD].reshape(
            stretch_count, CTOK, HD
        )
        scores = (
            jnp.einsum("ctd,csd->cts", query_h, keys_h, preferred_element_type=jnp.float32) * scale
        )
        scores = jnp.where(causal, scores, -jnp.inf)
        peak = jnp.max(scores, axis=-1, keepdims=True)
        expo = jnp.exp(scores - peak)
        weights = (expo / jnp.sum(expo, axis=-1, keepdims=True)).astype(jnp.bfloat16)
        result = jnp.einsum("cts,csd->ctd", weights, vals_h, preferred_element_type=jnp.float32)
        prefill_parts.append(result.astype(jnp.bfloat16).reshape(token_rows_local, HD))
    prefill_heads = jnp.concatenate(prefill_parts, axis=1)
    ctx_keys, ctx_vals = (
        lax.all_gather(keys_mine[:token_rows_local], "section", axis=0, tiled=True),
        lax.all_gather(vals_mine[:token_rows_local], "section", axis=0, tiled=True),
    )
    self_keys = keys_mine[token_rows_local:]
    self_vals = vals_mine[token_rows_local:]
    tok_total = ctx_keys.shape[0]
    page_count = tok_total // PAGE
    match = decode_page_table[:, :, None] == jnp.arange(page_count, dtype=jnp.int32)[None, None, :]
    present = jnp.any(match, axis=1)
    place = jnp.sum(jnp.where(match, jnp.arange(PPR, dtype=jnp.int32)[None, :, None], 0), axis=1)
    keypos = place[:, :, None] * PAGE + jnp.arange(PAGE, dtype=jnp.int32)[None, None, :]
    live = (present[:, :, None] & (keypos < lengths[:, None, None])).reshape(row_here, tok_total)
    outs = []
    for i in range(heads_here):
        which = i // group
        query_h = query_dec[:, i * HD : (i + 1) * HD]
        scores = (
            jnp.einsum("rd,nd->rn", query_h, ctx_keys, preferred_element_type=jnp.float32) * scale
        )
        own_score = (
            jnp.sum(query_h.astype(jnp.float32) * self_keys.astype(jnp.float32), axis=-1) * scale
        )
        weights, own_weight = softmax_with_own(scores, live, own_score)
        result = jnp.dot(weights, ctx_vals, preferred_element_type=jnp.float32)
        result = result + own_weight.astype(jnp.float32)[:, None] * self_vals.astype(jnp.float32)
        outs.append(result.astype(jnp.bfloat16))
    decode_heads = jnp.concatenate(outs, axis=1)
    return (prefill_heads, decode_heads)


def solution(mesh):
    placed = (
        P(("parts", "section"), "tensor"),
        P(("parts", "section"), "tensor"),
        P(None, "tensor"),
        P(None, "tensor"),
        P("tensor", None, None),
        P(),
        P(("parts", "section")),
        P(("parts", "section"), None),
        P(("parts", "section")),
    )
    return jax.shard_map(
        on_device,
        mesh=mesh,
        in_specs=placed,
        out_specs=(P(("parts", "section"), "tensor"), P(("parts", "section"), "tensor")),
        check_vma=False,
    )
```

profile of v0, /device:TPU:4, one launch (start us, length us, event | category | flops | bytes accessed | tf_op | source)
XLA Modules:
  0.0 686.2 jit_solution(4720152892462717632)
XLA Ops:
  28.0 6.9 %select_bitcast_fusion.3 = (bf16[8192,128]{1,0:T(8,128)(2,1)}, bf16[8192,128]{1,0:T(8,128)(2,1)}, bf16[8192,128]{1,0:T(8,128)(2,1)}, bf16[8192,128]{1,0:T(8,128)(2,1)}) fusion(bf16[2,8192,128]{2,1,0:T(8,128)(2,1)} %param.13, s32[]{:T(128)S(6)} %select_n.168, pred[]{:T(512)S(6)} %eq.30, s32[]{:T(128)S(6)} %select_n.176, pred[]{:T(512)S(6)} %eq.31, ...), kind=kLoop, calls=%fused_computation.41 | loop fusion | flops 4194304 | bytes 16777236 | tf_op jit(solution)/shard_map/jit(_where)/select_n | solution.py:22
  35.0 100.5 %all-gather.4.cloned.1.call-done = bf16[512,8192]{1,0:T(8,128)(2,1)} async-done(((bf16[512,1024]{1,0:T(8,128)(2,1)}), bf16[512,8192]{1,0:T(8,128)(2,1)}) %all-gather.4.cloned.1.call-update) | async-done | bytes 8388624 | tf_op jit(solution)/shard_map/all_gather | solution.py:78
  135.4 7.6 %constant_dynamic-update-slice_fusion.1 = bf16[1024,8192]{1,0:T(8,128)(2,1)} fusion(bf16[512,8192]{1,0:T(8,128)(2,1)} %all-gather.4.cloned.1.call-done), kind=kLoop, calls=%fused_computation.173 | loop fusion | bytes 16777216
  143.0 117.7 %all-gather.6.cloned.1.call-done = bf16[512,8192]{1,0:T(8,128)(2,1)} async-done(((bf16[512,1024]{1,0:T(8,128)(2,1)}), bf16[512,8192]{1,0:T(8,128)(2,1)}) %all-gather.6.cloned.1.call-update) | async-done | bytes 8388624 | tf_op jit(solution)/shard_map/all_gather | solution.py:79
  260.8 7.6 %constant_dynamic-update-slice_fusion = bf16[1024,8192]{1,0:T(8,128)(2,1)} fusion(bf16[1024,8192]{1,0:T(8,128)(2,1)} %constant_dynamic-update-slice_fusion.1, bf16[512,8192]{1,0:T(8,128)(2,1)} %all-gather.6.cloned.1.call-done), kind=kLoop, calls=%fused_computation.172 | loop fusion | bytes 16777216 | tf_op jit(solution)/shard_map/concatenate | solution.py:76
  268.3 13.3 %convolution_convert_fusion = bf16[1024,256]{1,0:T(8,128)(2,1)} fusion(bf16[1024,8192]{1,0:T(8,128)(2,1)} %constant_dynamic-update-slice_fusion, bf16[8192,256]{1,0:T(8,128)(2,1)} %param.12), kind=kOutput, calls=%fused_computation.52 | convolution fusion | flops 4295229440 | bytes 21495808 | tf_op jit(solution)/shard_map/dot_general | solution.py:84
  283.5 1.6 add.214
  285.1 1.9 copy.67
  287.7 249.4 %all-reduce.4.cloned.1.call-done = (bf16[8192,128]{1,0:T(8,128)(2,1)}, bf16[8192,128]{1,0:T(8,128)(2,1)}, bf16[8192,128]{1,0:T(8,128)(2,1)}, bf16[8192,128]{1,0:T(8,128)(2,1)}) async-done(((bf16[8192,128]{1,0:T(8,128)(2,1)}, bf16[8192,128]{1,0:T(8,128)(2,1)}, bf16[8192,128]{1,0:T(8,128)(2,1)}, bf16[8192,128]{1,0:T(8,128)(2,1)}), (bf16[8192,128]{1,0:T(8,128)(2,1)}, bf16[8192,128]{1,0:T(8,128)(2,1)}, ...) | async-done | bytes 8388624 | tf_op jit(solution)/shard_map/psum | solution.py:23
  537.0 1.1 constant_dynamic-slice_fusion.2
  538.3 0.9 copy.57
  539.1 1.2 constant_dynamic-slice_fusion.4
  540.3 0.8 copy.56
  541.3 1.2 pad_maximum_fusion
  542.9 33.4 %all-reduce.5 = bf16[4,128,64]{1,2,0:T(8,128)(2,1)S(1)} all-reduce(f32[4,128,64]{1,2,0:T(8,128)S(1)} %convolution_bitcast_fusion), channel_id=1, replica_groups=mesh['parts'=2,'tensor'=8,'section'=2] {'tensor'}, use_global_device_ids=true, to_apply=%region_4.5 | all-reduce | flops 32768 | bytes 196608 | tf_op jit(solution)/shard_map/psum | solution.py:71
  576.8 22.3 %fusion.121 = (bf16[1024,1024]{1,0:T(8,128)(2,1)S(1)}, f32[1024,1024]{1,0:T(8,128)S(1)}) fusion(bf16[1024,8192]{1,0:T(8,128)(2,1)} %constant_dynamic-update-slice_fusion, bf16[8192,1024]{1,0:T(8,128)(2,1)} %param.11), kind=kOutput, calls=%fused_computation.247 | convolution fusion | flops 17180917760 | bytes 39845888 | tf_op jit(solution)/shard_map/dot_general | solution.py:83
  599.6 0.9 fusion.110
  600.5 15.2 %all-gather.8.cloned.1.call-done = bf16[1024,2048]{1,0:T(8,128)(2,1)} async-done(((bf16[1024,256]{1,0:T(8,128)(2,1)}), bf16[1024,2048]{1,0:T(8,128)(2,1)}) %all-gather.8.cloned.1.call-update) | async-done | bytes 4194320 | tf_op jit(solution)/shard_map/all_gather | solution.py:92
  615.7 1.0 constant_dynamic-slice_fusion
  616.7 2.0 all_gather.18
  618.7 2.4 fusion.122
  621.2 2.4 fusion.123
  623.5 2.4 fusion.124
  625.9 2.4 fusion.125
  628.4 2.4 fusion.126
  630.8 2.4 fusion.127
  633.2 2.5 fusion.128
  635.7 2.1 fusion.129
  638.7 2.3 all_gather.19
  641.0 1.6 convolution_convert_fusion.8
  642.6 1.6 constant_dynamic-update-slice_fusion.9
  645.1 0.9 convolution_convert_fusion.7
  646.9 0.9 convolution_convert_fusion.6
  648.7 0.9 convolution_convert_fusion.5
  650.6 0.9 convolution_convert_fusion.4
  652.4 0.9 convolution_convert_fusion.3
  654.2 0.9 convolution_convert_fusion.2
  655.8 2.1 fusion.68
  658.0 2.2 fusion.11
  666.5 1.5 fusion.44
  668.0 1.5 fusion.46
  669.5 1.5 fusion.48
  671.0 1.5 fusion.50
  672.6 1.5 fusion.52
  674.1 1.5 fusion.54
  675.6 1.5 fusion.56
  677.1 1.5 fusion.58
  678.7 1.0 copy-done.27
  (122 shorter events, 19.9 us)
Async XLA Ops:
  7.2 1.6 copy-start.25
  7.2 9.9 %copy-start.24 = (s32[16]{0:T(128)S(1)}, s32[16]{0:T(128)}, u32[]{:S(2)}) copy-start(s32[16]{0:T(128)} %param.14) | copy-start | bytes 196
  7.2 128.3 %all-gather.4.cloned.1.call-start = ((), (), s32[]{:S(2)}) async-start(), calls=%async_computation | async-start | bytes 9437184 | tf_op jit(solution)/shard_map/all_gather | solution.py:78
  7.9 252.8 %all-gather.6.cloned.1.call-start = ((), (), s32[]{:S(2)}) async-start(), calls=%async_computation.1 | async-start | bytes 9437184 | tf_op jit(solution)/shard_map/all_gather | solution.py:79
  8.7 528.4 %all-reduce.4.cloned.1.call-start = ((), (), s32[]{:S(2)}) async-start(), calls=%async_computation.3 | async-start | bytes 16777216 | tf_op jit(solution)/shard_map/psum | solution.py:23
  34.9 580.8 %all-gather.8.cloned.1.call-start = ((), (), s32[]{:S(2)}) async-start(), calls=%async_computation.2 | async-start | bytes 4718592 | tf_op jit(solution)/shard_map/all_gather | solution.py:92
  268.3 13.3 %copy-start.12 = (s32[512,32]{0,1:T(8,128)S(1)}, s32[512,32]{0,1:T(8,128)}, u32[]{:S(2)}) copy-start(s32[512,32]{0,1:T(8,128)} %param.16) | copy-start | bytes 196612
  285.1 2.1 copy-start.26
  539.1 3.3 copy-start.7
  599.1 34.1 %copy-start.8 = (bf16[1024,1024]{1,0:T(8,128)(2,1)}, bf16[1024,1024]{1,0:T(8,128)(2,1)S(1)}, u32[]{:S(2)}) copy-start(bf16[1024,1024]{1,0:T(8,128)(2,1)S(1)} %get-tuple-element.52) | copy-start | bytes 6291460
  635.7 2.1 copy-start.11
  637.8 6.4 copy-start.10
  638.0 8.0 %copy-start.9 = (bf16[512,128]{1,0:T(8,128)(2,1)S(1)}, bf16[512,128]{1,0:T(8,128)(2,1)}, u32[]{:S(2)}) copy-start(bf16[512,128]{1,0:T(8,128)(2,1)} %get-tuple-element.25) | copy-start | bytes 393220
  655.4 2.5 copy-start.20
  655.4 2.5 copy-start.21
  655.8 4.4 copy-start.5
  657.9 2.8 copy-start.18
  658.0 2.8 copy-start.19
  658.0 2.8 copy-start.4
  660.2 1.6 copy-start.3
  660.8 1.5 copy-start.16
  660.8 1.5 copy-start.17
  660.8 1.8 copy-start.2
  661.8 1.7 copy-start.1
  662.6 1.5 copy-start.14
  662.6 1.5 copy-start.15
  662.6 1.8 copy-start
  664.3 1.2 copy-start.22
  664.8 1.7 copy-start.6
  664.8 1.7 copy-start.13
  665.9 2.1 copy-start.23
  678.6 1.0 copy-start.27
Sparse Core Ops, SparseCore 0:
  10.2 125.1 all-gather.3
  137.6 123.0 all-gather.5
  265.3 271.6 all-reduce.3
  539.5 76.1 all-gather.7
where the time goes:
time: 689 us; the launch traced here: 686 us
  waiting for transfers between devices  484 us (70%)
  matrix products  76.9 us (11%)
  blocking collectives  37.7 us (5%)
  between operations  32.4 us (5%)
  local copies, waits for them, and re-layouts  32.1 us (5%)
  other arithmetic  22.8 us (3%)
    psum x1, waiting for transfers between devices, broadcast(): return lax.psum(block, axis)  249 us
    all_gather x1, waiting for transfers between devices, on_device(): lax.all_gather(decode_hidden_rows, 'tensor', axis=1, tiled=True)  118 us
    all_gather x1, waiting for transfers between devices, on_device(): lax.all_gather(tokens, 'tensor', axis=1, tiled=True)  100 us
    psum x1, blocking collectives, on_device(): low_rank = lax.psum(low_part, 'tensor').astype(jnp.bfloat16)  33.4 us
    dot_general x1, matrix products, on_device(): jnp.dot(rows_all, query_matrix, preferred_element_type=jnp.float32)  22.3 us
    dot_general x8, matrix products, on_device(): jnp.einsum('rd,nd->rn', query_h, ctx_keys, preferred_element_type=jnp.flo...  19 us
    all_gather x1, waiting for transfers between devices, on_device(): keyval_all = lax.all_gather(keyval_mine, 'tensor', axis=1, tiled=True)  15.2 us
  transfers between devices with their start and end apart: 4, of which 4 were waited for; matrix products, arithmetic and copies ran while one was open for 11% of the time, Pallas kernels for 0%

commit v1 on v0

v1 whole, which is shorter than its diff:
```python
import functools
import math

import jax
import jax.numpy as jnp
from jax import lax
from jax.experimental import pallas as pl
from jax.experimental.pallas import tpu as pltpu
from jax.sharding import PartitionSpec as P

HQ = 64
KVH = 8
HD = 128
ADAPTER_RANK = 64
CTOK = 128
POOL_PER_INDEX = 2
PAGE = 16
PPR = 32
ADAPTER_SCALE = 2.0
SCALE = 1.0 / math.sqrt(HD)
GROUP = HQ // KVH


def dot_t(a, b):
    return lax.dot_general(a, b, (((1,), (1,)), ((), ())), preferred_element_type=jnp.float32)


def attention_kernel(qt, qd, kt, vt, kc, vc, ks, vs, bias, out_t, out_d):
    causal = lax.broadcasted_iota(jnp.int32, (CTOK, CTOK), 0) >= lax.broadcasted_iota(
        jnp.int32, (CTOK, CTOK), 1
    )
    for c in range(qt.shape[0] // CTOK):
        rows = pl.ds(c * CTOK, CTOK)
        scores = jnp.where(causal, dot_t(qt[rows, :], kt[rows, :]) * SCALE, -jnp.inf)
        expo = jnp.exp(scores - jnp.max(scores, axis=-1, keepdims=True))
        weights = (expo / jnp.sum(expo, axis=-1, keepdims=True)).astype(jnp.bfloat16)
        result = jnp.dot(weights, vt[rows, :], preferred_element_type=jnp.float32)
        out_t[rows, :] = result.astype(jnp.bfloat16)
    tile = min(128, qd.shape[0])
    for r in range(qd.shape[0] // tile):
        rows = pl.ds(r * tile, tile)
        query = qd[rows, :]
        scores = dot_t(query, kc[...]) * SCALE + bias[rows, :].astype(jnp.float32)
        own = (
            jnp.sum(
                query.astype(jnp.float32) * ks[rows, :].astype(jnp.float32), axis=-1, keepdims=True
            )
            * SCALE
        )
        top = jnp.maximum(jnp.max(scores, axis=-1, keepdims=True), own)
        expo = jnp.exp(scores - top)
        own_exp = jnp.exp(own - top)
        total = jnp.sum(expo, axis=-1, keepdims=True) + own_exp
        weights = (expo / total).astype(jnp.bfloat16)
        own_weight = (own_exp / total).astype(jnp.bfloat16).astype(jnp.float32)
        result = jnp.dot(weights, vc[...], preferred_element_type=jnp.float32)
        result = result + own_weight * vs[rows, :].astype(jnp.float32)
        out_d[rows, :] = result.astype(jnp.bfloat16)


def attention(query_tok, query_dec, keys_tok, vals_tok, keys_ctx, vals_ctx, self_k, self_v, bias):
    heads = query_tok.shape[1] // HD

    def per_head(rows):
        return pl.BlockSpec((rows, HD), lambda i: (0, i))

    def per_group(array):
        return pl.BlockSpec((array.shape[0], HD), lambda i: (0, i // GROUP))

    shared = (keys_tok, vals_tok, keys_ctx, vals_ctx, self_k, self_v)
    return pl.pallas_call(
        attention_kernel,
        grid=(heads,),
        in_specs=[
            per_head(query_tok.shape[0]),
            per_head(query_dec.shape[0]),
            *[per_group(a) for a in shared],
            pl.BlockSpec(bias.shape, lambda i: (0, 0)),
        ],
        out_specs=[per_head(query_tok.shape[0]), per_head(query_dec.shape[0])],
        out_shape=[
            jax.ShapeDtypeStruct(query_tok.shape, jnp.bfloat16),
            jax.ShapeDtypeStruct(query_dec.shape, jnp.bfloat16),
        ],
        compiler_params=pltpu.CompilerParams(vmem_limit_bytes=32 * 1024 * 1024),
    )(query_tok, query_dec, *shared, bias)


def live_bias(decode_page_table, lengths, page_count):
    match = decode_page_table[:, :, None] == jnp.arange(page_count, dtype=jnp.int32)[None, None, :]
    place = jnp.max(jnp.where(match, jnp.arange(PPR, dtype=jnp.int32)[None, :, None], -1), axis=1)
    left = jnp.where(place >= 0, lengths[:, None] - place * PAGE, 0)
    live = jnp.arange(PAGE, dtype=jnp.int32)[None, None, :] < left[:, :, None]
    bias = jnp.where(live, 0.0, -jnp.inf).astype(jnp.bfloat16)
    return bias.reshape(lengths.shape[0], page_count * PAGE)


def own_heads(keyval_mine, heads_here):
    index = lax.axis_index("tensor")
    if heads_here == GROUP and keyval_mine.shape[1] == 2 * HD:
        half = KVH // 2
        first, second = keyval_mine[:, :HD], keyval_mine[:, HD:]
        holds_keys = index < half
        one = lax.ppermute(
            jnp.where(holds_keys, first, second),
            "tensor",
            [(j, 2 * j) for j in range(half)] + [(half + j, 2 * j + 1) for j in range(half)],
        )
        two = lax.ppermute(
            jnp.where(holds_keys, second, first),
            "tensor",
            [(j, 2 * j + 1) for j in range(half)] + [(half + j, 2 * j) for j in range(half)],
        )
        even = index % 2 == 0
        return jnp.where(even, one, two), jnp.where(even, two, one)
    kv_here = max(1, heads_here // GROUP)
    whole = lax.all_gather(keyval_mine, "tensor", axis=1, tiled=True)
    first = index * heads_here // GROUP
    return (
        lax.dynamic_slice_in_dim(whole, first * HD, kv_here * HD, 1),
        lax.dynamic_slice_in_dim(whole, (KVH + first) * HD, kv_here * HD, 1),
    )


def on_device(
    tokens,
    decode_hidden_rows,
    query_matrix,
    key_value_matrix,
    adapter_slot_pool,
    adapter_slot_map,
    tenant_adapter_index,
    decode_page_table,
    lengths,
):
    token_rows = tokens.shape[0]
    heads_here = query_matrix.shape[1] // HD
    stretches = token_rows // CTOK
    index = lax.axis_index("tensor")
    slots = adapter_slot_map[tenant_adapter_index]

    up = jnp.swapaxes(adapter_slot_pool[:, :, ADAPTER_RANK:], 1, 2)
    up_all = lax.all_to_all(up, "tensor", split_axis=2, concat_axis=0, tiled=True)
    tokens_all = lax.all_gather(tokens, "tensor", axis=1, tiled=True)
    rows_all = lax.all_gather(decode_hidden_rows, "tensor", axis=1, tiled=True)

    low_local = jnp.einsum(
        "td,sdr->str",
        tokens_all,
        adapter_slot_pool[:, :, :ADAPTER_RANK],
        preferred_element_type=jnp.float32,
    )
    query_sum = jnp.dot(tokens_all, query_matrix, preferred_element_type=jnp.float32)
    keyval_tok = jnp.dot(tokens_all, key_value_matrix, preferred_element_type=jnp.float32)
    query_dec = jnp.dot(rows_all, query_matrix, preferred_element_type=jnp.float32)
    keyval_dec = jnp.dot(rows_all, key_value_matrix, preferred_element_type=jnp.float32)

    low_local = low_local.reshape(POOL_PER_INDEX, stretches, CTOK, ADAPTER_RANK)
    held = index * POOL_PER_INDEX + jnp.arange(POOL_PER_INDEX, dtype=jnp.int32)
    mine = held[:, None] == slots[None, :]
    low_mine = jnp.sum(jnp.where(mine[:, :, None, None], low_local, 0.0), axis=0)
    low = lax.psum(low_mine.astype(jnp.bfloat16), "tensor")
    update = jnp.einsum("ctr,crd->ctd", low, up_all[slots], preferred_element_type=jnp.float32)
    update = update.reshape(token_rows, query_matrix.shape[1])
    query_tok = (query_sum + ADAPTER_SCALE * update).astype(jnp.bfloat16)

    keyval_mine = jnp.concatenate((keyval_tok, keyval_dec), axis=0).astype(jnp.bfloat16)
    keys, vals = own_heads(keyval_mine, heads_here)
    keys_ctx = lax.all_gather(keys[:token_rows], "section", axis=0, tiled=True)
    vals_ctx = lax.all_gather(vals[:token_rows], "section", axis=0, tiled=True)
    bias = live_bias(decode_page_table, lengths, keys_ctx.shape[0] // PAGE)
    return tuple(
        attention(
            query_tok,
            query_dec.astype(jnp.bfloat16),
            keys[:token_rows],
            vals[:token_rows],
            keys_ctx,
            vals_ctx,
            keys[token_rows:],
            vals[token_rows:],
            bias,
        )
    )


def solution(mesh):
    placed = (
        P(("parts", "section"), "tensor"),
        P(("parts", "section"), "tensor"),
        P(None, "tensor"),
        P(None, "tensor"),
        P("tensor", None, None),
        P(),
        P(("parts", "section")),
        P(("parts", "section"), None),
        P(("parts", "section")),
    )
    return jax.shard_map(
        on_device,
        mesh=mesh,
        in_specs=placed,
        out_specs=(P(("parts", "section"), "tensor"), P(("parts", "section"), "tensor")),
        check_vma=False,
    )
```

time: 689 us -> 435 us (0.63)
  waiting for transfers between devices: 484 us -> 254 us
  local copies, waits for them, and re-layouts: 32.1 us -> 68 us
  blocking collectives: 37.7 us -> 3.98 us
  Pallas kernels: 0 us -> 27.4 us
  matrix products: 76.9 us -> 50.7 us
  other arithmetic: 22.8 us -> 3.71 us
  between operations: 32.4 us -> 14 us
  starting transfers between devices: 0.16 us -> 11.7 us
    psum x1, waiting for transfers between devices: 249 us -> 50.3 us  [on_device(): low = lax.psum(low_mine.astype(jnp.bfloat16), 'tensor')]
    all_gather x3 -> x2, waiting for transfers between devices: 233 us -> 106 us  [the longest x1 106 us: on_device(): rows_all = lax.all_gather(decode_hidden_rows, 'tensor', axis=1, tiled=True)]
    all_to_all x0 -> x1, waiting for transfers between devices: none -> 95.7 us  [on_device(): lax.all_to_all(up, 'tensor', split_axis=2, concat_axis=0, tiled=True)]
    unnamed x64 -> x19, local copies, waits for them, and re-layouts: 12.7 us -> 48.1 us
    psum x1 -> x0, blocking collectives: 33.4 us -> none  [on_device(): low_rank = lax.psum(low_part, 'tensor').astype(jnp.bfloat16)]
    pallas_call x0 -> x1, Pallas kernels: none -> 27.4 us  [attention(): pl.pallas_call(attention_kernel, grid=(heads,), in_specs=[per_head(query_...]
    dot_general x34 -> x4, matrix products: 41.3 us -> 30.9 us  [the longest x1 15 us: on_device(): jnp.dot(tokens_all, query_matrix, preferred_element_type=jnp.float32)]
    dot_general x1, matrix products: 22.3 us -> 12.7 us  [on_device(): jnp.dot(rows_all, query_matrix, preferred_element_type=jnp.float32)]
  transfers between devices with their start and end apart: 4 -> 6, of which waited for: 4 -> 3; matrix products, arithmetic and copies ran while one was open for 11% -> 28% of each run, Pallas kernels for 0% -> 0%
where the time goes in v1:
time: 435 us; the launch traced here: 433 us
  waiting for transfers between devices  254 us (58%)
  local copies, waits for them, and re-layouts  68 us (16%)
  matrix products  50.7 us (12%)
  Pallas kernels  27.4 us (6%)
  between operations  14 us (3%)
  starting transfers between devices  11.7 us (3%)
    all_gather x1, waiting for transfers between devices, on_device(): rows_all = lax.all_gather(decode_hidden_rows, 'tensor', axis=1, tiled=True)  106 us
    all_to_all x1, waiting for transfers between devices, on_device(): lax.all_to_all(up, 'tensor', split_axis=2, concat_axis=0, tiled=True)  95.7 us
    psum x1, waiting for transfers between devices, on_device(): low = lax.psum(low_mine.astype(jnp.bfloat16), 'tensor')  50.3 us
    unnamed x19, local copies, waits for them, and re-layouts  48.1 us
    pallas_call x1, Pallas kernels, attention(): pl.pallas_call(attention_kernel, grid=(heads,), in_specs=[per_head(query_...  27.4 us
    dot_general x1, matrix products, on_device(): jnp.dot(tokens_all, query_matrix, preferred_element_type=jnp.float32)  15 us
    dot_general x1, matrix products, on_device(): jnp.dot(rows_all, query_matrix, preferred_element_type=jnp.float32)  12.7 us
    all_to_all x1, local copies, waits for them, and re-layouts, on_device(): lax.all_to_all(up, 'tensor', split_axis=2, concat_axis=0, tiled=True)  9.09 us
  transfers between devices with their start and end apart: 6, of which 3 were waited for; matrix products, arithmetic and copies ran while one was open for 28% of the time, Pallas kernels for 0%

profile of v1, /device:TPU:4, one launch (start us, length us, event | category | flops | bytes accessed | tf_op | source)
XLA Modules:
  0.0 433.0 jit_solution(11153326340939801138)
XLA Ops:
  7.2 0.0 copy-start
  7.2 0.0 all-gather.3.cloned.1.call-start
  7.2 0.7 all-gather.3.cloned.1.call-update
  7.9 0.0 all-gather.5.cloned.1.call-start
  8.0 0.7 all-gather.5.cloned.1.call-update
  8.7 3.4 slice.27
  12.0 35.4 %copy.48 = bf16[2,8192,64]{2,0,1:T(2,128)(2,1)} copy(bf16[2,8192,64]{2,1,0:T(8,128)(2,1)S(1)} %slice.27) | data formatting | bytes 4194304
  47.5 7.6 %reshape.97 = bf16[8,2,65536]{2,1,0:T(2,128)(2,1)} reshape(bf16[8192,2,64]{2,1,0:T(2,128)(2,1)} %bitcast.54) | data formatting | bytes 4194304
  55.0 6.3 %all-to-all-start = ((bf16[8,2,65536]{2,1,0:T(2,128)(2,1)}), bf16[8,2,65536]{2,1,0:T(2,128)(2,1)S(1)}, u32[]{:S(2)}, u32[]{:S(2)}) async-start(bf16[8,2,65536]{2,1,0:T(2,128)(2,1)} %reshape.97), calls=%async_computation | async-start | bytes 4194304 | tf_op jit(solution)/shard_map/all_to_all | solution.py:143
  61.4 0.0 all-reduce.2.cloned.1.call-start
  61.4 0.0 copy-done.6
  61.4 0.0 copy-done
  61.4 0.6 gather_fusion
  62.1 0.1 broadcast_compare_fusion
  62.1 0.1 broadcast_bitcast_fusion
  62.2 0.0 copy-done.3
  62.2 0.6 select_reduce_fusion
  62.9 1.6 lt.49
  64.5 3.0 copy.35
  67.5 0.1 lt.47
  67.6 1.8 select_convert_fusion.bias
  69.5 95.7 %all-to-all-done = bf16[8,2,65536]{2,1,0:T(2,128)(2,1)S(1)} async-done(((bf16[8,2,65536]{2,1,0:T(2,128)(2,1)}), bf16[8,2,65536]{2,1,0:T(2,128)(2,1)S(1)}, u32[]{:S(2)}, u32[]{:S(2)}) %all-to-all-start) | async-done | bytes 2097184 | tf_op jit(solution)/shard_map/all_to_all | solution.py:143
  165.2 5.0 %reshape.98 = bf16[8192,2,64]{2,1,0:T(2,128)(2,1)} reshape(bf16[8,2,65536]{2,1,0:T(2,128)(2,1)S(1)} %all-to-all-done) | data formatting | bytes 4194304
  170.2 9.1 %copy.37 = bf16[2,64,8,1024]{3,1,0,2:T(8,128)(2,1)S(1)} copy(bf16[2,64,8,1024]{1,0,3,2:T(2,128)(2,1)} %bitcast.53) | data formatting | bytes 4194304 | tf_op jit(solution)/shard_map/all_to_all | solution.py:143
  179.3 1.4 gather_fusion.1
  180.7 7.7 %fusion.9 = bf16[64,512]{1,0:T(8,128)(2,1)S(1)} fusion(bf16[512,8192]{1,0:T(8,128)(2,1)} %all-gather.3.cloned.1.call-done, bf16[2,8192,128]{2,1,0:T(8,128)(2,1)} %param.13, pred[2,512]{1,0:T(4,128)(4,1)S(1)} %bitcast.57), kind=kOutput, calls=%fused_computation.16 | convolution fusion | flops 1073840128 | bytes 12649472 | tf_op jit(solution)/shard_map/td,sdr->str/dot_general | solution.py:147
  188.4 0.6 copy_bitcast_fusion.1
  189.0 0.0 all-reduce.2.cloned.1.call-update
  189.1 6.9 %convolution_convert_fusion.2 = bf16[512,256]{1,0:T(8,128)(2,1)S(1)} fusion(bf16[512,8192]{1,0:T(8,128)(2,1)} %all-gather.3.cloned.1.call-done, bf16[8192,256]{1,0:T(8,128)(2,1)} %param.12), kind=kOutput, calls=%fused_computation.14 | convolution fusion | flops 2147614720 | bytes 12845056 | tf_op jit(solution)/shard_map/dot_general | solution.py:154
  196.0 106.3 %all-gather.5.cloned.1.call-done = bf16[512,8192]{1,0:T(8,128)(2,1)} async-done(((bf16[512,1024]{1,0:T(8,128)(2,1)}), bf16[512,8192]{1,0:T(8,128)(2,1)}) %all-gather.5.cloned.1.call-update) | async-done | bytes 8388624 | tf_op jit(solution)/shard_map/all_gather | solution.py:145
  302.3 7.0 %convolution_convert_fusion.1 = bf16[512,256]{1,0:T(8,128)(2,1)S(1)} fusion(bf16[512,8192]{1,0:T(8,128)(2,1)} %all-gather.5.cloned.1.call-done, bf16[8192,256]{1,0:T(8,128)(2,1)} %param.12), kind=kOutput, calls=%fused_computation.13 | convolution fusion | flops 2147614720 | bytes 12845056 | tf_op jit(solution)/shard_map/dot_general | solution.py:156
  309.3 0.1 broadcast_select_fusion
  309.4 0.1 collective-permute-start.1
  309.5 0.0 copy-start.2
  309.5 5.2 %collective-permute-start = (bf16[1024,128]{1,0:T(8,128)(2,1)S(1)}, bf16[1024,128]{1,0:T(8,128)(2,1)}, u32[]{:S(2)}, u32[]{:S(2)}) collective-permute-start(bf16[1024,128]{1,0:T(8,128)(2,1)S(1)} %get-tuple-element.5), channel_id=1, source_target_pairs={{0,0},{2,4},{4,8},{6,12},{8,2},{10,6},{12,10},{14,14},{1,1},{3,5},... | collective-permute-start | bytes 786440 | tf_op jit(solution)/shard_map/ppermute | solution.py:104
  314.7 0.0 copy-done.5
  314.7 12.7 %convolution_convert_fusion.qd = bf16[512,1024]{1,0:T(8,128)(2,1)S(1)} fusion(bf16[512,8192]{1,0:T(8,128)(2,1)S(1)} %copy-done.5, bf16[8192,1024]{1,0:T(8,128)(2,1)} %param.11), kind=kOutput, calls=%fused_computation.12 | convolution fusion | flops 8590458880 | bytes 26214400 | tf_op jit(solution)/shard_map/dot_general | solution.py:155
  327.5 50.3 %all-reduce.2.cloned.1.call-done = bf16[4,128,64]{1,2,0:T(8,128)(2,1)} async-done(((bf16[4,128,64]{1,2,0:T(8,128)(2,1)}), bf16[4,128,64]{1,2,0:T(8,128)(2,1)}) %all-reduce.2.cloned.1.call-update) | async-done | bytes 65552 | tf_op jit(solution)/shard_map/psum | solution.py:162
  377.7 1.3 convolution_multiply_fusion
  379.0 0.0 copy-start.1
  379.1 15.0 %fusion.3.qt = bf16[512,1024]{1,0:T(8,128)(2,1)S(1)} fusion(f32[4,128,1024]{2,1,0:T(8,128)S(1)} %convolution_multiply_fusion, bf16[512,8192]{1,0:T(8,128)(2,1)} %all-gather.3.cloned.1.call-done, bf16[8192,1024]{1,0:T(8,128)(2,1)} %param.11), kind=kOutput, calls=%fused_computation.9 | convolution fusion | flops 8590983168 | bytes 28311552 | tf_op jit(solution)/shard_map/dot_general | solution.py:153
  394.0 0.0 collective-permute-done.1
  394.1 0.0 collective-permute-done
  394.1 1.0 broadcast_select_fusion.2
  395.1 2.0 all_gather.14.kc
  397.1 2.0 all_gather.15.vc
  399.1 27.4 %shard_map.104 = (bf16[512,1024]{1,0:T(8,128)(2,1)}, bf16[512,1024]{1,0:T(8,128)(2,1)}) custom-call(bf16[512,1024]{1,0:T(8,128)(2,1)S(1)} %fusion.3.qt, bf16[512,1024]{1,0:T(8,128)(2,1)S(1)} %convolution_convert_fusion.qd, bf16[512,128]{1,0:T(8,128)(2,1)S(1)} %get-tuple-element.9.kt, bf16[512,128]{1,0:T(8,128)(2,1)S(1)} %get-tuple-element.7.vt, ...), custom_call_target="tpu_custom_call" | custom-call | tf_op jit(solution)/shard_map/pallas_call | solution.py:71
  426.5 0.0 copy-done.1
  (17 shorter events, 0.1 us)
Async XLA Ops:
  7.2 54.2 %copy-start = (s32[16]{0:T(128)S(1)}, s32[16]{0:T(128)}, u32[]{:S(2)}) copy-start(s32[16]{0:T(128)} %param.14) | copy-start | bytes 196
  7.2 173.5 %all-gather.3.cloned.1.call-start = ((), (), s32[]{:S(2)}) async-start(), calls=%async_computation.1 | async-start | bytes 9437184 | tf_op jit(solution)/shard_map/all_gather | solution.py:144
  7.9 294.3 %all-gather.5.cloned.1.call-start = ((), (), s32[]{:S(2)}) async-start(), calls=%async_computation.3 | async-start | bytes 9437184 | tf_op jit(solution)/shard_map/all_gather | solution.py:145
  47.4 13.9 %copy-start.6 = (s32[4]{0:T(128)S(1)}, s32[4]{0:T(128)}, u32[]{:S(2)}) copy-start(s32[4]{0:T(128)} %param.15) | copy-start | bytes 52
  47.4 14.8 %copy-start.3 = (s32[512,32]{0,1:T(8,128)S(1)}, s32[512,32]{0,1:T(8,128)}, u32[]{:S(2)}) copy-start(s32[512,32]{0,1:T(8,128)} %param.16) | copy-start | bytes 196612
  47.4 15.4 %copy-start.4 = (s32[512]{0:T(512)S(1)}, s32[512]{0:T(512)}, u32[]{:S(2)}) copy-start(s32[512]{0:T(512)} %param.17) | copy-start | bytes 6148
  55.0 110.2 %all-to-all-start = ((bf16[8,2,65536]{2,1,0:T(2,128)(2,1)}), bf16[8,2,65536]{2,1,0:T(2,128)(2,1)S(1)}, u32[]{:S(2)}, u32[]{:S(2)}) async-start(bf16[8,2,65536]{2,1,0:T(2,128)(2,1)} %reshape.97), calls=%async_computation | async-start | bytes 4194304 | tf_op jit(solution)/shard_map/all_to_all | solution.py:143
  61.4 316.3 %all-reduce.2.cloned.1.call-start = ((), (), s32[]{:S(2)}) async-start(), calls=%async_computation.2 | async-start | bytes 131072 | tf_op jit(solution)/shard_map/psum | solution.py:162
  302.3 12.5 %copy-start.5 = (bf16[512,8192]{1,0:T(8,128)(2,1)S(1)}, bf16[512,8192]{1,0:T(8,128)(2,1)}, u32[]{:S(2)}) copy-start(bf16[512,8192]{1,0:T(8,128)(2,1)} %all-gather.5.cloned.1.call-done) | copy-start | bytes 25165828
  309.4 84.6 %collective-permute-start.1 = (bf16[1024,128]{1,0:T(8,128)(2,1)S(1)}, bf16[1024,128]{1,0:T(8,128)(2,1)S(1)}, u32[]{:S(2)}, u32[]{:S(2)}) collective-permute-start(bf16[1024,128]{1,0:T(8,128)(2,1)S(1)} %get-tuple-element.4), channel_id=1, source_target_pairs={{0,2},{2,6},{4,10},{6,14},{8,0},{10,4},{12,8},{14,12},{1,3},{3,7},... | collective-permute-start | bytes 786440 | tf_op jit(solution)/shard_map/ppermute | solution.py:109
  309.5 68.2 %copy-start.2 = (bf16[4,64,1024]{2,1,0:T(8,128)(2,1)S(1)}, bf16[4,64,1024]{2,1,0:T(8,128)(2,1)}, u32[]{:S(2)}) copy-start(bf16[4,64,1024]{2,1,0:T(8,128)(2,1)} %gather_fusion.1) | copy-start | bytes 1572868
  309.5 84.5 %collective-permute-start = (bf16[1024,128]{1,0:T(8,128)(2,1)S(1)}, bf16[1024,128]{1,0:T(8,128)(2,1)}, u32[]{:S(2)}, u32[]{:S(2)}) collective-permute-start(bf16[1024,128]{1,0:T(8,128)(2,1)S(1)} %get-tuple-element.5), channel_id=1, source_target_pairs={{0,0},{2,4},{4,8},{6,12},{8,2},{10,6},{12,10},{14,14},{1,1},{3,5},... | collective-permute-start | bytes 786440 | tf_op jit(solution)/shard_map/ppermute | solution.py:104
  379.0 47.5 %copy-start.1 = (s32[16]{0:T(128)S(1)}, s32[16]{0:T(128)}, u32[]{:S(2)}) copy-start(s32[16]{0:T(128)} %param.14) | copy-start | bytes 196
Sparse Core Ops, SparseCore 0:
  10.2 166.6 all-gather.2
  179.1 123.0 all-gather.4
  306.2 71.4 all-reduce.1

commit v2 on v1

--- a/solution.py
+++ b/solution.py
@@ -86,6 +86,248 @@
     )(query_tok, query_dec, *shared, bias)
 
 
+def link_orders():
+    sent, links, arrived = {}, {}, {z: [(0, (z, 0, 0)), (0, (z, 0, 1))] for z in range(4)}
+    events = [(0, z, (z, 0, h)) for h in range(2) for z in range(4)]
+    while events:
+        events.sort(key=lambda e: (e[0], e[2][1], abs(e[2][0] - e[1]), e[2][2], e[1]))
+        time, z, unit = events.pop(0)
+        source, side, half = unit
+        out = []
+        if side == 0:
+            if source <= z < 3:
+                out.append(("up", z + 1, unit, time))
+            if source >= z > 0:
+                out.append(("down", z - 1, unit, time))
+            if not (source == (z ^ 1) and half == 0):
+                out.append(("y", z, (source, 1, half), time))
+        elif source == z and half == 0:
+            way = "up" if (z ^ 1) > z else "down"
+            out.append(("ext", z ^ 1, (z, 1, 0), max(time, 4.5) if z in (1, 2) else time))
+        for kind, place, name, ready in out:
+            link = (z, place)
+            done = max(links.get(link, 0), ready) + 1
+            if kind != "ext" or z not in (1, 2):
+                links[link] = done
+            else:
+                done = 7
+            sent.setdefault((z, unit), []).append(kind)
+            arrived[place].append((done, name))
+            if kind != "ext":
+                events.append((done, place, name))
+    tables = []
+    for z in range(4):
+        order = [name for _, name in sorted(arrived[z], key=lambda e: (e[0], e[1][1]))]
+        last = max(i for i, u in enumerate(order) if {"up", "down"} & set(sent.get((z, u), [])))
+        row = []
+        for i, unit in enumerate(order):
+            kinds = sent.get((z, unit), [])
+            flags = sum(bit for kind, bit in (("up", 1), ("down", 2), ("y", 4)) if kind in kinds)
+            late = order.index((z, 1, 0))
+            if i == max(last, late):
+                flags += 8
+            row.append(flags * 16 + unit[0] * 4 + unit[1] * 2 + unit[2])
+        tables.append(row)
+    return tables
+
+
+def project_kernel(
+    tok, dec, wq, wkv, pool, q_out, kv_out, low_out, up_out,
+    x, w, wk, ad, up_send, up_all, local_sem, send_sem, recv_sem, up_ssem, up_rsem, pair_sem,
+):
+    tables = link_orders()
+    me = lax.axis_index("tensor")
+    core = lax.axis_index("section")
+    z, y = me // 2, me % 2
+    rows, width = tok.shape
+
+    own = [
+        pltpu.make_async_copy(tok, x.at[me, 0], local_sem.at[0]),
+        pltpu.make_async_copy(dec, x.at[me, 1], local_sem.at[1]),
+    ]
+    loads = [
+        pltpu.make_async_copy(pool, ad, local_sem.at[2]),
+        pltpu.make_async_copy(wkv, wk, local_sem.at[3]),
+        pltpu.make_async_copy(wq, w, local_sem.at[4]),
+    ]
+    for copy in own + loads:
+        copy.start()
+
+    barrier = pltpu.get_barrier_semaphore()
+    for k in range(1, 8):
+        pl.semaphore_signal(
+            barrier, inc=1, device_id={"tensor": (me + k) % 8}, device_id_type=pl.DeviceIdType.MESH
+        )
+    pl.semaphore_signal(
+        barrier, inc=1, device_id={"section": 1 - core}, device_id_type=pl.DeviceIdType.MESH
+    )
+    pl.semaphore_wait(barrier, 8)
+    for copy in own:
+        copy.wait()
+
+    def decode(i):
+        code = jnp.int32(0)
+        for place in range(4):
+            for step in range(16):
+                here = jnp.logical_and(z == place, i == step)
+                code = jnp.where(here, tables[place][step], code)
+        unit, flags = code % 16, code // 16
+        slot = (unit // 4) * 2 + (y + unit // 2) % 2
+        return slot, unit % 2, flags
+
+    def send(kind, slot, half, dest):
+        return pltpu.make_async_remote_copy(
+            src_ref=x.at[slot, half],
+            dst_ref=x.at[slot, half],
+            send_sem=send_sem.at[kind, slot, half],
+            recv_sem=recv_sem.at[slot, half],
+            device_id={"tensor": dest},
+            device_id_type=pl.DeviceIdType.MESH,
+        )
+
+    def passed_on(slot, half, flags):
+        near = (z // 2) * 2 + (1 - z % 2)
+        return (
+            (flags % 2 == 1, send(0, slot, half, me + 2)),
+            (flags // 2 % 2 == 1, send(1, slot, half, me - 2)),
+            (flags // 4 % 2 == 1, send(2, slot, half, z * 2 + 1 - y)),
+            (flags // 8 % 2 == 1, send(3, z * 2 + 1 - y, 0, near * 2 + y)),
+        )
+
+    def forward(i):
+        slot, half, flags = decode(i)
+        for wanted, copy in passed_on(slot, half, flags):
+            pl.when(wanted)(copy.start)
+
+    forward(jnp.int32(0))
+    forward(jnp.int32(1))
+
+    loads[0].wait()
+    eye = (
+        lax.broadcasted_iota(jnp.int32, (128, 128), 0)
+        == lax.broadcasted_iota(jnp.int32, (128, 128), 1)
+    ).astype(jnp.bfloat16)
+
+    def turn(j, carry):
+        block = ad[core, pl.ds(pl.multiple_of(j * width, width), width), :]
+        up_send[j] = dot_t(eye, block)[ADAPTER_RANK:, :].astype(jnp.bfloat16)
+        return carry
+
+    lax.fori_loop(0, 8, turn, 0)
+
+    def up_copy(k):
+        return pltpu.make_async_remote_copy(
+            src_ref=up_send.at[(me + k) % 8],
+            dst_ref=up_all.at[core, me],
+            send_sem=up_ssem.at[k],
+            recv_sem=up_rsem.at[k],
+            device_id={"tensor": (me + k) % 8},
+            device_id_type=pl.DeviceIdType.MESH,
+        )
+
+    for k in range(1, 8):
+        up_copy(k).start()
+    up_own = pltpu.make_async_copy(up_send.at[me], up_all.at[core, me], local_sem.at[5])
+    up_own.start()
+
+    q_out[...] = jnp.zeros_like(q_out)
+    kv_out[...] = jnp.zeros_like(kv_out)
+    low_out[...] = jnp.zeros_like(low_out)
+    loads[1].wait()
+    loads[2].wait()
+
+    def work(i, carry):
+        slot, half, flags = decode(i)
+
+        @pl.when(i >= 2)
+        def _():
+            send(0, slot, half, me).wait_recv()
+            for wanted, copy in passed_on(slot, half, flags):
+                pl.when(wanted)(copy.start)
+
+        block = x[slot, half]
+        depth = pl.ds(pl.multiple_of(slot * width, width), width)
+        here = pl.ds(pl.multiple_of(half * rows, rows), rows)
+        for c in range(0, q_out.shape[1], 256):
+            q_out[here, c : c + 256] += jnp.dot(
+                block, w[depth, c : c + 256], preferred_element_type=jnp.float32
+            )
+        kv_out[here, :] += jnp.dot(block, wk[depth, :], preferred_element_type=jnp.float32)
+
+        @pl.when(half == 0)
+        def _():
+            for k in range(POOL_PER_INDEX):
+                low_out[k] += jnp.dot(block, ad[k, depth, :], preferred_element_type=jnp.float32)
+
+        return carry
+
+    lax.fori_loop(0, 16, work, 0)
+
+    up_own.wait()
+    for k in range(1, 8):
+        up_copy(k).wait()
+    pair = pltpu.make_async_remote_copy(
+        src_ref=up_all.at[core],
+        dst_ref=up_all.at[core],
+        send_sem=pair_sem.at[0],
+        recv_sem=pair_sem.at[1],
+        device_id={"section": 1 - core},
+        device_id_type=pl.DeviceIdType.MESH,
+    )
+    pair.start()
+
+    def drain(i, carry):
+        slot, half, flags = decode(i)
+        for wanted, copy in passed_on(slot, half, flags):
+            pl.when(wanted)(copy.wait_send)
+        return carry
+
+    lax.fori_loop(0, 16, drain, 0)
+    pair.wait()
+    result = pltpu.make_async_copy(up_all, up_out, local_sem.at[6])
+    result.start()
+    result.wait()
+
+
+def project(tokens, decode_hidden_rows, query_matrix, key_value_matrix, pool):
+    rows, width = tokens.shape
+    cols, kv_cols = query_matrix.shape[1], key_value_matrix.shape[1]
+    depth = query_matrix.shape[0]
+    bf16, f32 = jnp.bfloat16, jnp.float32
+    whole = pl.BlockSpec(memory_space=pltpu.VMEM)
+    return pl.pallas_call(
+        project_kernel,
+        in_specs=[pl.BlockSpec(memory_space=pl.ANY)] * 5,
+        out_specs=[whole, whole, whole, pl.BlockSpec(memory_space=pl.ANY)],
+        out_shape=[
+            jax.ShapeDtypeStruct((2 * rows, cols), f32),
+            jax.ShapeDtypeStruct((2 * rows, kv_cols), f32),
+            jax.ShapeDtypeStruct((POOL_PER_INDEX, rows, 128), f32),
+            jax.ShapeDtypeStruct((2, 8, ADAPTER_RANK, width), bf16),
+        ],
+        scratch_shapes=[
+            pltpu.VMEM((8, 2, rows, width), bf16),
+            pltpu.VMEM((depth, cols), bf16),
+            pltpu.VMEM((depth, kv_cols), bf16),
+            pltpu.VMEM(pool.shape, bf16),
+            pltpu.VMEM((8, ADAPTER_RANK, width), bf16),
+            pltpu.VMEM((2, 8, ADAPTER_RANK, width), bf16),
+            pltpu.SemaphoreType.DMA((7,)),
+            pltpu.SemaphoreType.DMA((4, 8, 2)),
+            pltpu.SemaphoreType.DMA((8, 2)),
+            pltpu.SemaphoreType.DMA((8,)),
+            pltpu.SemaphoreType.DMA((8,)),
+            pltpu.SemaphoreType.DMA((2,)),
+        ],
+        compiler_params=pltpu.CompilerParams(
+            collective_id=0, has_side_effects=True, vmem_limit_bytes=60 * 1024 * 1024
+        ),
+        cost_estimate=pl.CostEstimate(
+            flops=4 * rows * depth * (cols + kv_cols), bytes_accessed=30 << 20, transcendentals=0
+        ),
+    )(tokens, decode_hidden_rows, query_matrix, key_value_matrix, pool)
+
+
 def live_bias(decode_page_table, lengths, page_count):
     match = decode_page_table[:, :, None] == jnp.arange(page_count, dtype=jnp.int32)[None, None, :]
     place = jnp.max(jnp.where(match, jnp.arange(PPR, dtype=jnp.int32)[None, :, None], -1), axis=1)
@@ -139,32 +381,43 @@
     index = lax.axis_index("tensor")
     slots = adapter_slot_map[tenant_adapter_index]
 
-    up = jnp.swapaxes(adapter_slot_pool[:, :, ADAPTER_RANK:], 1, 2)
-    up_all = lax.all_to_all(up, "tensor", split_axis=2, concat_axis=0, tiled=True)
-    tokens_all = lax.all_gather(tokens, "tensor", axis=1, tiled=True)
-    rows_all = lax.all_gather(decode_hidden_rows, "tensor", axis=1, tiled=True)
-
-    low_local = jnp.einsum(
-        "td,sdr->str",
-        tokens_all,
-        adapter_slot_pool[:, :, :ADAPTER_RANK],
-        preferred_element_type=jnp.float32,
-    )
-    query_sum = jnp.dot(tokens_all, query_matrix, preferred_element_type=jnp.float32)
-    keyval_tok = jnp.dot(tokens_all, key_value_matrix, preferred_element_type=jnp.float32)
-    query_dec = jnp.dot(rows_all, query_matrix, preferred_element_type=jnp.float32)
-    keyval_dec = jnp.dot(rows_all, key_value_matrix, preferred_element_type=jnp.float32)
+    linked = lax.axis_size("tensor") == 8 and lax.axis_size("section") == 2
+    if linked and heads_here == GROUP:
+        query_all, keyval_all, low_local, up_all = project(
+            tokens, decode_hidden_rows, query_matrix, key_value_matrix, adapter_slot_pool
+        )
+        query_sum, query_dec = query_all[:token_rows], query_all[token_rows:]
+        keyval_mine = keyval_all.astype(jnp.bfloat16)
+        low_local = low_local[:, :, :ADAPTER_RANK]
+        picked = up_all[slots % POOL_PER_INDEX, slots // POOL_PER_INDEX]
+    else:
+        up = jnp.swapaxes(adapter_slot_pool[:, :, ADAPTER_RANK:], 1, 2)
+        up_all = lax.all_to_all(up, "tensor", split_axis=2, concat_axis=0, tiled=True)
+        tokens_all = lax.all_gather(tokens, "tensor", axis=1, tiled=True)
+        rows_all = lax.all_gather(decode_hidden_rows, "tensor", axis=1, tiled=True)
+
+        low_local = jnp.einsum(
+            "td,sdr->str",
+            tokens_all,
+            adapter_slot_pool[:, :, :ADAPTER_RANK],
+            preferred_element_type=jnp.float32,
+        )
+        query_sum = jnp.dot(tokens_all, query_matrix, preferred_element_type=jnp.float32)
+        keyval_tok = jnp.dot(tokens_all, key_value_matrix, preferred_element_type=jnp.float32)
+        query_dec = jnp.dot(rows_all, query_matrix, preferred_element_type=jnp.float32)
+        keyval_dec = jnp.dot(rows_all, key_value_matrix, preferred_element_type=jnp.float32)
+        keyval_mine = jnp.concatenate((keyval_tok, keyval_dec), axis=0).astype(jnp.bfloat16)
+        picked = up_all[slots]
 
     low_local = low_local.reshape(POOL_PER_INDEX, stretches, CTOK, ADAPTER_RANK)
     held = index * POOL_PER_INDEX + jnp.arange(POOL_PER_INDEX, dtype=jnp.int32)
     mine = held[:, None] == slots[None, :]
     low_mine = jnp.sum(jnp.where(mine[:, :, None, None], low_local, 0.0), axis=0)
     low = lax.psum(low_mine.astype(jnp.bfloat16), "tensor")
-    update = jnp.einsum("ctr,crd->ctd", low, up_all[slots], preferred_element_type=jnp.float32)
+    update = jnp.einsum("ctr,crd->ctd", low, picked, preferred_element_type=jnp.float32)
     update = update.reshape(token_rows, query_matrix.shape[1])
     query_tok = (query_sum + ADAPTER_SCALE * update).astype(jnp.bfloat16)
 
-    keyval_mine = jnp.concatenate((keyval_tok, keyval_dec), axis=0).astype(jnp.bfloat16)
     keys, vals = own_heads(keyval_mine, heads_here)
     keys_ctx = lax.all_gather(keys[:token_rows], "section", axis=0, tiled=True)
     vals_ctx = lax.all_gather(vals[:token_rows], "section", axis=0, tiled=True)

time: 435 us -> 316 us (0.73)
  waiting for transfers between devices: 254 us -> 58.6 us
  Pallas kernels: 27.4 us -> 217 us
  local copies, waits for them, and re-layouts: 68 us -> 9.06 us
  matrix products: 50.7 us -> 1.32 us
  starting transfers between devices: 11.7 us -> 1.95 us
  other arithmetic: 3.71 us -> 8.07 us
    pallas_call x0 -> x1, Pallas kernels: none -> 190 us  [project(): pl.pallas_call(project_kernel, in_specs=[pl.BlockSpec(memory_space=pl.ANY...]
    all_gather x2 -> x0, waiting for transfers between devices: 106 us -> none  [the longest x1 106 us: on_device(): rows_all = lax.all_gather(decode_hidden_rows, 'tensor', axis=1, tiled=True)]
    all_to_all x1 -> x0, waiting for transfers between devices: 95.7 us -> none  [on_device(): lax.all_to_all(up, 'tensor', split_axis=2, concat_axis=0, tiled=True)]
    dot_general x6 -> x1, matrix products: 50.7 us -> 1.32 us  [on_device(): jnp.einsum('ctr,crd->ctd', low, picked, preferred_element_type=jnp.float32)]
    unnamed x19 -> x8, local copies, waits for them, and re-layouts: 48.1 us -> 0.11 us
    all_to_all x1 -> x0, local copies, waits for them, and re-layouts: 9.09 us -> none  [on_device(): lax.all_to_all(up, 'tensor', split_axis=2, concat_axis=0, tiled=True)]
    psum x1, waiting for transfers between devices: 50.3 us -> 58.5 us  [on_device(): low = lax.psum(low_mine.astype(jnp.bfloat16), 'tensor')]
    all_to_all x1 -> x0, starting transfers between devices: 6.33 us -> none  [on_device(): lax.all_to_all(up, 'tensor', split_axis=2, concat_axis=0, tiled=True)]
  transfers between devices with their start and end apart: 6 -> 3, of which waited for: 3 -> 1; matrix products, arithmetic and copies ran while one was open for 28% -> 4% of each run, Pallas kernels for 0% -> 0%
where the time goes in v2:
time: 316 us; the launch traced here: 314 us
  Pallas kernels  217 us (69%)
  waiting for transfers between devices  58.6 us (19%)
  between operations  14.2 us (4%)
  local copies, waits for them, and re-layouts  9.06 us (3%)
  other arithmetic  8.07 us (3%)
  blocking collectives  3.98 us (1%)
    pallas_call x1, Pallas kernels, project(): pl.pallas_call(project_kernel, in_specs=[pl.BlockSpec(memory_space=pl.ANY...  190 us
    psum x1, waiting for transfers between devices, on_device(): low = lax.psum(low_mine.astype(jnp.bfloat16), 'tensor')  58.5 us
    pallas_call x1, Pallas kernels, attention(): pl.pallas_call(attention_kernel, grid=(heads,), in_specs=[per_head(query_...  27.4 us
  transfers between devices with their start and end apart: 3, of which 1 were waited for; matrix products, arithmetic and copies ran while one was open for 4% of the time, Pallas kernels for 0%

profile of v2, /device:TPU:4, one launch (start us, length us, event | category | flops | bytes accessed | tf_op | source)
XLA Modules:
  0.0 314.3 jit_solution(13940118665171999344)
XLA Ops:
  7.2 0.0 copy-start
  7.2 0.0 all-reduce.2.cloned.1.call-start
  7.2 0.7 compare_select_fusion.2
  7.9 0.0 copy-done
  7.9 0.6 gather_fusion
  8.5 0.1 broadcast_compare_fusion
  8.6 0.1 broadcast_bitcast_fusion
  8.7 189.7 %shard_map.104 = (f32[1024,1024]{1,0:T(8,128)}, f32[1024,256]{1,0:T(8,128)}, f32[2,512,128]{2,1,0:T(8,128)}, bf16[2,8,64,1024]{3,2,1,0:T(8,128)(2,1)}) custom-call(bf16[512,1024]{1,0:T(8,128)(2,1)} %tok.1, bf16[512,1024]{1,0:T(8,128)(2,1)} %dec.1, bf16[8192,1024]{1,0:T(8,128)(2,1)} %wq.1, bf16[8192,256]{1,0:T(8,128)(2,1)} %wkv.1, bf16[2,8192,128]{2,1,0:T(8,128)(2,1)} %pool.1), custom_call_target="tpu_custom_call" | custom-call | flops 21474836480 | bytes 31457280 | tf_op jit(solution)/shard_map/pallas_call | solution.py:298
  198.4 0.0 copy-start.1
  198.4 0.0 copy-start.2
  198.4 1.3 select_reduce_fusion.1
  199.7 0.1 copy.22
  199.8 0.6 copy_bitcast_fusion
  200.5 0.0 all-reduce.2.cloned.1.call-update
  200.5 1.3 convert_element_type.20
  201.8 0.8 broadcast_select_fusion
  202.6 0.0 collective-permute-start.1
  202.6 1.9 collective-permute-start
  204.5 0.0 copy-done.1
  204.5 0.6 select_reduce_fusion
  205.2 0.0 copy-done.2
  205.2 1.6 lt.67
  206.8 1.9 copy.24
  208.7 0.1 lt.65
  208.8 0.3 select_convert_fusion.bias
  209.1 1.8 slice.57.qd
  210.9 2.2 gather_fusion.1
  213.1 58.5 %all-reduce.2.cloned.1.call-done = bf16[4,128,64]{1,2,0:T(8,128)(2,1)} async-done(((bf16[4,128,64]{1,2,0:T(8,128)(2,1)}), bf16[4,128,64]{1,2,0:T(8,128)(2,1)}) %all-reduce.2.cloned.1.call-update) | async-done | bytes 65552 | tf_op jit(solution)/shard_map/psum | solution.py:416
  271.6 1.3 convolution_multiply_fusion
  272.9 2.0 fusion.qt
  275.0 0.0 collective-permute-done.1
  275.0 0.0 collective-permute-done
  275.0 1.0 broadcast_select_fusion.2
  276.0 2.0 all_gather.6.kc
  278.0 2.0 all_gather.7.vc
  280.0 27.4 %shard_map.105 = (bf16[512,1024]{1,0:T(8,128)(2,1)}, bf16[512,1024]{1,0:T(8,128)(2,1)}) custom-call(bf16[512,1024]{1,0:T(8,128)(2,1)S(1)} %fusion.qt, bf16[512,1024]{1,0:T(8,128)(2,1)S(1)} %slice.57.qd, bf16[512,128]{1,0:T(8,128)(2,1)S(1)} %get-tuple-element.17.kt, bf16[512,128]{1,0:T(8,128)(2,1)S(1)} %get-tuple-element.15.vt, ...), custom_call_target="tpu_custom_call" | custom-call | tf_op jit(solution)/shard_map/pallas_call | solution.py:71
  (8 shorter events, 0.1 us)
Async XLA Ops:
  7.2 0.7 copy-start
  7.2 264.4 %all-reduce.2.cloned.1.call-start = ((), (), s32[]{:S(2)}) async-start(), calls=%async_computation | async-start | bytes 131072 | tf_op jit(solution)/shard_map/psum | solution.py:416
  198.4 6.1 %copy-start.1 = (s32[512,32]{0,1:T(8,128)S(1)}, s32[512,32]{0,1:T(8,128)}, u32[]{:S(2)}) copy-start(s32[512,32]{0,1:T(8,128)} %param.16) | copy-start | bytes 196612
  198.4 6.8 %copy-start.2 = (s32[512]{0:T(512)S(1)}, s32[512]{0:T(512)}, u32[]{:S(2)}) copy-start(s32[512]{0:T(512)} %param.17) | copy-start | bytes 6148
  202.6 72.4 %collective-permute-start.1 = (bf16[1024,128]{1,0:T(8,128)(2,1)}, bf16[1024,128]{1,0:T(8,128)(2,1)S(1)}, u32[]{:S(2)}, u32[]{:S(2)}) collective-permute-start(bf16[1024,128]{1,0:T(8,128)(2,1)} %get-tuple-element.12), channel_id=1, source_target_pairs={{0,2},{2,6},{4,10},{6,14},{8,0},{10,4},{12,8},{14,12},{1,3},{3,7},... | collective-permute-start | bytes 786440 | tf_op jit(solution)/shard_map/ppermute | solution.py:351
  202.6 72.4 %collective-permute-start = (bf16[1024,128]{1,0:T(8,128)(2,1)}, bf16[1024,128]{1,0:T(8,128)(2,1)}, u32[]{:S(2)}, u32[]{:S(2)}) collective-permute-start(bf16[1024,128]{1,0:T(8,128)(2,1)} %get-tuple-element.13), channel_id=1, source_target_pairs={{0,0},{2,4},{4,8},{6,12},{8,2},{10,6},{12,10},{14,14},{1,1},{3,5},... | collective-permute-start | bytes 786440 | tf_op jit(solution)/shard_map/ppermute | solution.py:346
Sparse Core Ops, SparseCore 0:
  200.6 70.9 all-reduce.1

commit v3 on v1

--- a/solution.py
+++ b/solution.py
@@ -86,6 +86,472 @@
     )(query_tok, query_dec, *shared, bias)
 
 
+SHARED = (0, 2)
+QUARTERS = 4
+
+
+def link_orders():
+    arrived = {z: {(z, 0, q): 0 for q in range(QUARTERS)} for z in range(4)}
+    waiting = {(z, way): [] for z in range(4) for way in range(3)}
+    sent = {z: [] for z in range(4)}
+
+    def reach(z, unit, time):
+        source, side, q = unit
+        if side == 0:
+            if source <= z < 3:
+                waiting[z, 0].append((q, time, abs(source - z), unit))
+            if source >= z > 0:
+                waiting[z, 1].append((q, time, abs(source - z), unit))
+            if not (source == (z ^ 1) and q in SHARED):
+                waiting[z, 2].append((q, time, abs(source - z), unit))
+        elif source == z and q in SHARED:
+            waiting[z, 0 if (z ^ 1) > z else 1].append((q, time, 9, unit))
+
+    for z in range(4):
+        for q in range(QUARTERS):
+            reach(z, (z, 0, q), 0)
+    for time in range(64):
+        landed = []
+        for (z, way), queue in waiting.items():
+            if queue:
+                best = min(queue)
+                queue.remove(best)
+                unit = best[3]
+                sent[z].append((time, way, unit))
+                place = (z + 1, z - 1, z)[way]
+                landed.append((place, (unit[0], 1, unit[2]) if way == 2 else unit))
+        for place, unit in landed:
+            arrived[place][unit] = time + 1
+            reach(place, unit, time + 1)
+    tables = []
+    for z in range(4):
+        order = sorted(arrived[z], key=lambda u: (arrived[z][u], u[2], u[1], abs(u[0] - z), u))
+        times = [arrived[z][u] for u in order]
+        issue = [[] for _ in order]
+        for time, way, unit in sorted(sent[z]):
+            early = max([0] + [i for i in range(len(order)) if times[i] <= time - 1])
+            step = max(early, order.index(unit))
+            issue[step].append(64 + way * 16 + unit[0] * 4 + unit[2] + 128 * unit[1])
+        prefill_ready = max(order.index(u) for u in order if u[2] < 2)
+        decode_ready = max(order.index(u) for u in order if u[2] == 2)
+        jobs = []
+        for j in range(JOBS):
+            step = jobs[-1] + 1 if jobs else prefill_ready
+            jobs.append(min(31, max(step, decode_ready) if j == 6 else step))
+        units = [u[0] * 8 + u[1] * 4 + u[2] for u in order]
+        done = [sum(at <= i for at in jobs) for i in range(32)]
+        tables.append((units, issue, done))
+    return tables
+
+
+JOBS = 12
+
+
+def serve_kernel(
+    slot_core, slot_index, held, tok, dec, wq, wkv, pool, bias,
+    out_t, out_d,
+    x, w, wk, ad, acc, acc_kv, acc_low, up_send, up_all, query, kv_send, ctx, own_kv, low_send, low_all,
+    local_sem, send_sem, recv_sem, up_ssem, up_rsem, pair_sem,
+    kv_ssem, kv_rsem, kv_lsem, ctx_ssem, ctx_rsem, low_ssem, low_rsem,
+):
+    tables = link_orders()
+    mesh_id = pl.DeviceIdType.MESH
+    me = lax.axis_index("tensor")
+    core = lax.axis_index("section")
+    z, y = me // 2, me % 2
+    rows, width = tok.shape
+    part = x.shape[2]
+    heads = wq.shape[1] // HD
+
+    own = [
+        pltpu.make_async_copy(
+            (tok, dec)[q // 2].at[pl.ds(q % 2 * part, part), :], x.at[me, q], local_sem.at[q]
+        )
+        for q in range(QUARTERS)
+    ]
+    loads = [
+        pltpu.make_async_copy(pool, ad, local_sem.at[4]),
+        pltpu.make_async_copy(wkv, wk, local_sem.at[5]),
+        pltpu.make_async_copy(wq, w, local_sem.at[6]),
+    ]
+    for copy in own + loads:
+        copy.start()
+
+    barrier = pltpu.get_barrier_semaphore()
+    for k in range(1, 8):
+        pl.semaphore_signal(
+            barrier, inc=1, device_id={"tensor": (me + k) % 8}, device_id_type=mesh_id
+        )
+    pl.semaphore_signal(barrier, inc=1, device_id={"section": 1 - core}, device_id_type=mesh_id)
+    pl.semaphore_wait(barrier, 8)
+    for copy in own:
+        copy.wait()
+
+    def look(i, values):
+        code = jnp.int32(0)
+        flat = z * 32 + i
+        for place in range(4):
+            for step in range(32):
+                if values[place][step]:
+                    code = jnp.where(flat == place * 32 + step, values[place][step], code)
+        return code
+
+    most = max(len(issue) for _, issues, _ in tables for issue in issues)
+
+    def send(way, slot, q, dest):
+        return pltpu.make_async_remote_copy(
+            src_ref=x.at[slot, q],
+            dst_ref=x.at[slot, q],
+            send_sem=send_sem.at[way, slot, q],
+            recv_sem=recv_sem.at[slot, q],
+            device_id={"tensor": dest},
+            device_id_type=mesh_id,
+        )
+
+    def passed_on(i):
+        out = []
+        for group in range(0, most, 3):
+            word = look(
+                i,
+                [
+                    [sum(c << (8 * k) for k, c in enumerate(issue[group : group + 3])) for issue in issues]
+                    for _, issues, _ in tables
+                ],
+            )
+            for k in range(min(3, most - group)):
+                code = word // (1 << (8 * k)) % 256
+                way = code // 16 % 4
+                side = code // 128
+                slot = code // 4 % 4 * 2 + (y + side) % 2
+                dest = jnp.where(way == 0, me + 2, jnp.where(way == 1, me - 2, z * 2 + 1 - y))
+                out.append((code > 0, send(way, slot, code % 4, dest)))
+        return out
+
+    def forward(i):
+        for wanted, copy in passed_on(i):
+            pl.when(wanted)(copy.start)
+
+    forward(jnp.int32(0))
+
+    loads[0].wait()
+    eye = (
+        lax.broadcasted_iota(jnp.int32, (128, 128), 0)
+        == lax.broadcasted_iota(jnp.int32, (128, 128), 1)
+    ).astype(jnp.bfloat16)
+
+    def turn(j, carry):
+        block = ad[core, pl.ds(pl.multiple_of(j * width, width), width), :]
+        up_send[j] = dot_t(eye, block)[ADAPTER_RANK:, :].astype(jnp.bfloat16)
+        return carry
+
+    lax.fori_loop(0, 8, turn, 0)
+
+    def peer_copy(src, dst, ssem, rsem, k):
+        return pltpu.make_async_remote_copy(
+            src_ref=src,
+            dst_ref=dst,
+            send_sem=ssem.at[k],
+            recv_sem=rsem.at[k],
+            device_id={"tensor": (me + k) % 8},
+            device_id_type=mesh_id,
+        )
+
+    def up_copy(k):
+        return peer_copy(up_send.at[(me + k) % 8], up_all.at[core, me], up_ssem, up_rsem, k)
+
+    def low_copy(k):
+        return peer_copy(low_send, low_all.at[k], low_ssem, low_rsem, k)
+
+    def to_core(ref, ssem, rsem):
+        return pltpu.make_async_remote_copy(
+            src_ref=ref,
+            dst_ref=ref,
+            send_sem=ssem,
+            recv_sem=rsem,
+            device_id={"section": 1 - core},
+            device_id_type=mesh_id,
+        )
+
+    for k in range(1, 8):
+        up_copy(k).start()
+    up_own = pltpu.make_async_copy(up_send.at[me], up_all.at[core, me], local_sem.at[7])
+    up_own.start()
+
+    acc[...] = jnp.zeros_like(acc)
+    acc_kv[...] = jnp.zeros_like(acc_kv)
+    acc_low[...] = jnp.zeros_like(acc_low)
+    loads[1].wait()
+    loads[2].wait()
+
+    kind = me // 4
+    stages = ((0, rows), (rows, part), (rows + part, part))
+
+    def kv_place(stage, which):
+        first, count = stages[stage]
+        if stage == 0:
+            return ctx.at[core, which]
+        return own_kv.at[which, pl.ds(first - rows, count), :]
+
+    def kv_copies(stage):
+        first, count = stages[stage]
+        for h in range(2):
+            dest = me % 4 * 2 + h
+            src = kv_send.at[h, pl.ds(first, count), :]
+            remote = pltpu.make_async_remote_copy(
+                src_ref=src,
+                dst_ref=kv_place(stage, kind),
+                send_sem=kv_ssem.at[stage, h],
+                recv_sem=kv_rsem.at[stage, kind],
+                device_id={"tensor": dest},
+                device_id_type=mesh_id,
+            )
+            local = pltpu.make_async_copy(src, kv_place(stage, kind), kv_lsem.at[stage])
+            yield dest, remote, local
+
+    def kv_start(stage):
+        first, count = stages[stage]
+        here = pl.ds(first, count)
+        for h in range(2):
+            kv_send[h, here, :] = acc_kv[here, h * HD : (h + 1) * HD].astype(jnp.bfloat16)
+        for dest, remote, local in kv_copies(stage):
+            pl.when(dest != me)(remote.start)
+
+            @pl.when(dest == me)
+            def _(local=local):
+                local.start()
+                local.wait()
+
+    def kv_wait(stage):
+        first, count = stages[stage]
+        for which in range(2):
+            arrival = pltpu.make_async_remote_copy(
+                src_ref=kv_send.at[0, pl.ds(first, count), :],
+                dst_ref=kv_place(stage, which),
+                send_sem=kv_ssem.at[stage, 0],
+                recv_sem=kv_rsem.at[stage, which],
+                device_id={"tensor": me},
+                device_id_type=mesh_id,
+            )
+            pl.when(which * 4 + me // 2 != me)(arrival.wait_recv)
+
+    def tokens_send():
+        kv_start(0)
+        packed = []
+        for c in range(rows // CTOK):
+            here = pl.ds(c * CTOK, CTOK)
+            low = jnp.zeros((CTOK, 128), jnp.float32)
+            for k in range(POOL_PER_INDEX):
+                r = k * (rows // CTOK) + c
+                low = low + jnp.where(held[r : r + 1, :] > 0.0, acc_low[k, here, :], 0.0)
+            packed.append(low)
+        lane = lax.broadcasted_iota(jnp.int32, (CTOK, 128), 1)
+        half = len(packed) // 2
+        for c in range(half):
+            other = pltpu.roll(packed[half + c], ADAPTER_RANK, 1)
+            both = jnp.where(lane < ADAPTER_RANK, packed[c], other)
+            low_send[pl.ds(c * CTOK, CTOK), :] = both.astype(jnp.bfloat16)
+        for k in range(1, 8):
+            low_copy(k).start()
+
+    def tokens_receive():
+        up_own.wait()
+        for k in range(1, 8):
+            up_copy(k).wait()
+        pair = to_core(up_all.at[core], pair_sem.at[0], pair_sem.at[1])
+        pair.start()
+        kv_wait(0)
+        to_core(ctx.at[core], ctx_ssem, ctx_rsem).start()
+        low = low_send[...].astype(jnp.float32)
+        for k in range(1, 8):
+            low_copy(k).wait()
+            low = low + low_all[k].astype(jnp.float32)
+        low = low.astype(jnp.bfloat16)
+        pair.wait()
+        half = rows // CTOK // 2
+        for c in range(rows // CTOK):
+            piece = low[c % half * CTOK : (c % half + 1) * CTOK, :]
+            piece = piece[:, c // half * ADAPTER_RANK : (c // half + 1) * ADAPTER_RANK]
+            update = jnp.dot(
+                piece, up_all[slot_core[c], slot_index[c]], preferred_element_type=jnp.float32
+            )
+            here = pl.ds(c * CTOK, CTOK)
+            query[here, :] = (acc[here, :] + ADAPTER_SCALE * update).astype(jnp.bfloat16)
+
+    causal = lax.broadcasted_iota(jnp.int32, (CTOK, CTOK), 0) >= lax.broadcasted_iota(
+        jnp.int32, (CTOK, CTOK), 1
+    )
+
+    def prefill_head(head):
+        cols = pl.ds(pl.multiple_of(head * HD, HD), HD)
+        for c in range(rows // CTOK):
+            here = pl.ds(c * CTOK, CTOK)
+            scores = dot_t(query[here, cols], ctx[core, 0, here, :]) * SCALE
+            scores = jnp.where(causal, scores, -jnp.inf)
+            expo = jnp.exp(scores - jnp.max(scores, axis=-1, keepdims=True))
+            weights = expo / jnp.sum(expo, axis=-1, keepdims=True)
+            result = jnp.dot(
+                weights.astype(jnp.bfloat16), ctx[core, 1, here, :], preferred_element_type=jnp.float32
+            )
+            out_t[here, cols] = result.astype(jnp.bfloat16)
+
+    def decode_head(head, first):
+        cols = pl.ds(pl.multiple_of(head * HD, HD), HD)
+        tile = 128
+        for r in range(first, first + part, tile):
+            here = pl.ds(r, tile)
+            q = acc[pl.ds(rows + r, tile), cols].astype(jnp.bfloat16)
+            scores = []
+            for s in range(2):
+                mask = bias[here, s * rows : (s + 1) * rows].astype(jnp.float32)
+                scores.append(dot_t(q, ctx[s, 0]) * SCALE + mask)
+            self_k = own_kv[0, here, :].astype(jnp.float32)
+            mine = jnp.sum(q.astype(jnp.float32) * self_k, axis=-1, keepdims=True) * SCALE
+            top = jnp.max(jnp.maximum(scores[0], scores[1]), axis=-1, keepdims=True)
+            top = jnp.maximum(top, mine)
+            expo = [jnp.exp(score - top) for score in scores]
+            mine = jnp.exp(mine - top)
+            inverse = 1.0 / (jnp.sum(expo[0] + expo[1], axis=-1, keepdims=True) + mine)
+            weight = (mine * inverse).astype(jnp.bfloat16).astype(jnp.float32)
+            result = weight * own_kv[1, here, :].astype(jnp.float32)
+            for s in range(2):
+                result = result + jnp.dot(
+                    (expo[s] * inverse).astype(jnp.bfloat16),
+                    ctx[s, 1],
+                    preferred_element_type=jnp.float32,
+                )
+            out_d[here, cols] = result.astype(jnp.bfloat16)
+
+    def job(j, carry):
+        pl.when(j == 0)(tokens_send)
+        pl.when(j == 1)(tokens_receive)
+
+        @pl.when(jnp.logical_and(j >= 2, j < 6))
+        def _():
+            prefill_head((j - 2) * 2)
+            prefill_head((j - 2) * 2 + 1)
+
+        pl.when(j == 6)(lambda: kv_start(1))
+
+        @pl.when(j == 7)
+        def _():
+            kv_wait(1)
+            to_core(ctx.at[core], ctx_ssem, ctx_rsem).wait()
+
+        @pl.when(j >= 8)
+        def _():
+            decode_head((j - 8) * 2, 0)
+            decode_head((j - 8) * 2 + 1, 0)
+
+        return carry
+
+    unit_table = [units for units, _, _ in tables]
+    done_table = [done for _, _, done in tables]
+
+    def work(i, done):
+        unit = look(i, unit_table)
+        slot, q = unit // 8 * 2 + (y + unit // 4) % 2, unit % 4
+
+        pl.when(slot != me)(send(0, slot, q, me).wait_recv)
+        pl.when(i > 0)(lambda: forward(i))
+
+        block = x[slot, q]
+        depth = pl.ds(pl.multiple_of(slot * width, width), width)
+        here = pl.ds(pl.multiple_of(q * part, part), part)
+        for c in range(0, acc.shape[1], 256):
+            acc[here, c : c + 256] += jnp.dot(
+                block, w[depth, c : c + 256], preferred_element_type=jnp.float32
+            )
+        acc_kv[here, :] += jnp.dot(block, wk[depth, :], preferred_element_type=jnp.float32)
+
+        @pl.when(q < 2)
+        def _():
+            for k in range(POOL_PER_INDEX):
+                acc_low[k, here, :] += jnp.dot(
+                    block, ad[k, depth, :], preferred_element_type=jnp.float32
+                )
+
+        until = look(i, done_table)
+        lax.fori_loop(done, until, job, 0)
+        return until
+
+    lax.fori_loop(0, 32, work, jnp.int32(0))
+
+    kv_start(2)
+
+    def drain(i, carry):
+        for wanted, copy in passed_on(i):
+            pl.when(wanted)(copy.wait_send)
+        return carry
+
+    lax.fori_loop(0, 32, drain, 0)
+    kv_wait(2)
+
+    def last(head, carry):
+        decode_head(head, part)
+        return carry
+
+    lax.fori_loop(0, heads, last, 0)
+    for stage in range(3):
+        for dest, remote, local in kv_copies(stage):
+            pl.when(dest != me)(remote.wait_send)
+
+
+def serve(slots, held, tokens, decode_hidden_rows, query_matrix, key_value_matrix, pool, bias):
+    rows, width = tokens.shape
+    depth, cols = query_matrix.shape
+    kv_cols = key_value_matrix.shape[1]
+    bf16, f32 = jnp.bfloat16, jnp.float32
+    vmem = pl.BlockSpec(memory_space=pltpu.VMEM)
+    smem = pl.BlockSpec(memory_space=pltpu.SMEM)
+    hbm = pl.BlockSpec(memory_space=pl.ANY)
+    dma = pltpu.SemaphoreType.DMA
+    return pl.pallas_call(
+        serve_kernel,
+        in_specs=[smem, smem, vmem] + [hbm] * 5 + [vmem],
+        out_specs=[vmem, vmem],
+        out_shape=[jax.ShapeDtypeStruct((rows, cols), bf16)] * 2,
+        scratch_shapes=[
+            pltpu.VMEM((8, QUARTERS, rows // 2, width), bf16),
+            pltpu.VMEM((depth, cols), bf16),
+            pltpu.VMEM((depth, kv_cols), bf16),
+            pltpu.VMEM(pool.shape, bf16),
+            pltpu.VMEM((2 * rows, cols), f32),
+            pltpu.VMEM((2 * rows, kv_cols), f32),
+            pltpu.VMEM((POOL_PER_INDEX, rows, 128), f32),
+            pltpu.VMEM((8, ADAPTER_RANK, width), bf16),
+            pltpu.VMEM((2, 8, ADAPTER_RANK, width), bf16),
+            pltpu.VMEM((rows, cols), bf16),
+            pltpu.VMEM((2, 2 * rows, HD), bf16),
+            pltpu.VMEM((2, 2, rows, HD), bf16),
+            pltpu.VMEM((2, rows, HD), bf16),
+            pltpu.VMEM((rows // 2, 128), bf16),
+            pltpu.VMEM((8, rows // 2, 128), bf16),
+            dma((8,)),
+            dma((3, 8, QUARTERS)),
+            dma((8, QUARTERS)),
+            dma((8,)),
+            dma((8,)),
+            dma((2,)),
+            dma((3, 2)),
+            dma((3, 2)),
+            dma((3,)),
+            dma,
+            dma,
+            dma((8,)),
+            dma((8,)),
+        ],
+        compiler_params=pltpu.CompilerParams(
+            collective_id=0, has_side_effects=True, vmem_limit_bytes=62 * 1024 * 1024
+        ),
+        cost_estimate=pl.CostEstimate(
+            flops=4 * rows * depth * (cols + kv_cols), bytes_accessed=30 << 20, transcendentals=0
+        ),
+    )(
+        slots % POOL_PER_INDEX, slots // POOL_PER_INDEX, held,
+        tokens, decode_hidden_rows, query_matrix, key_value_matrix, pool, bias,
+    )
+
+
 def live_bias(decode_page_table, lengths, page_count):
     match = decode_page_table[:, :, None] == jnp.arange(page_count, dtype=jnp.int32)[None, None, :]
     place = jnp.max(jnp.where(match, jnp.arange(PPR, dtype=jnp.int32)[None, :, None], -1), axis=1)
@@ -139,6 +605,25 @@
     index = lax.axis_index("tensor")
     slots = adapter_slot_map[tenant_adapter_index]
 
+    linked = lax.axis_size("tensor") == 8 and lax.axis_size("section") == 2
+    if linked and heads_here == GROUP:
+        bias = live_bias(decode_page_table, lengths, 2 * token_rows // PAGE)
+        here = index * POOL_PER_INDEX + jnp.arange(POOL_PER_INDEX, dtype=jnp.int32)
+        mine = (here[:, None] == slots[None, :]).astype(jnp.float32).reshape(-1, 1)
+        mine = jnp.broadcast_to(mine, (mine.shape[0], 128))
+        return tuple(
+            serve(
+                slots,
+                mine,
+                tokens,
+                decode_hidden_rows,
+                query_matrix,
+                key_value_matrix,
+                adapter_slot_pool,
+                bias,
+            )
+        )
+
     up = jnp.swapaxes(adapter_slot_pool[:, :, ADAPTER_RANK:], 1, 2)
     up_all = lax.all_to_all(up, "tensor", split_axis=2, concat_axis=0, tiled=True)
     tokens_all = lax.all_gather(tokens, "tensor", axis=1, tiled=True)

time: 435 us -> 247 us (0.57)
  waiting for transfers between devices: 254 us -> 0 us
  Pallas kernels: 27.4 us -> 232 us
  local copies, waits for them, and re-layouts: 68 us -> 9.53 us
  matrix products: 50.7 us -> 0 us
  between operations: 14 us -> 0.67 us
  starting transfers between devices: 11.7 us -> 0 us
    pallas_call x1, Pallas kernels: 27.4 us -> 232 us  [serve(): pl.pallas_call(serve_kernel, in_specs=[smem, smem, vmem] + [hbm] * 5 + [v...]
    all_gather x2 -> x0, waiting for transfers between devices: 106 us -> none  [the longest x1 106 us: on_device(): rows_all = lax.all_gather(decode_hidden_rows, 'tensor', axis=1, tiled=True)]
    all_to_all x1 -> x0, waiting for transfers between devices: 95.7 us -> none  [on_device(): lax.all_to_all(up, 'tensor', split_axis=2, concat_axis=0, tiled=True)]
    dot_general x6 -> x0, matrix products: 50.7 us -> none  [the longest x1 15 us: on_device(): jnp.dot(tokens_all, query_matrix, preferred_element_type=jnp.float32)]
    psum x1 -> x0, waiting for transfers between devices: 50.3 us -> none  [on_device(): low = lax.psum(low_mine.astype(jnp.bfloat16), 'tensor')]
    unnamed x19 -> x4, local copies, waits for them, and re-layouts: 48.1 us -> 4.53 us
    all_to_all x1 -> x0, local copies, waits for them, and re-layouts: 9.09 us -> none  [on_device(): lax.all_to_all(up, 'tensor', split_axis=2, concat_axis=0, tiled=True)]
    all_to_all x1 -> x0, starting transfers between devices: 6.33 us -> none  [on_device(): lax.all_to_all(up, 'tensor', split_axis=2, concat_axis=0, tiled=True)]
  transfers between devices with their start and end apart: 6 -> 0, of which waited for: 3 -> 0; matrix products, arithmetic and copies ran while one was open for 28% -> 0% of each run, Pallas kernels for 0% -> 0%
where the time goes in v3:
time: 247 us
  Pallas kernels  232 us (94%)
  local copies, waits for them, and re-layouts  9.53 us (4%)
  other arithmetic  4.73 us (2%)
    pallas_call x1, Pallas kernels, serve(): pl.pallas_call(serve_kernel, in_specs=[smem, smem, vmem] + [hbm] * 5 + [v...  232 us

profile of v3, /device:TPU:4, one launch (start us, length us, event | category | flops | bytes accessed | tf_op | source)
XLA Modules:
  0.0 246.9 jit_solution(3805443993217869052)
XLA Ops:
  0.6 0.0 copy-start
  0.6 0.7 compare_select_fusion
  1.3 0.0 copy-done
  1.3 0.6 gather_fusion
  2.0 0.6 and_select_fusion
  2.5 0.1 compare_convert_fusion
  2.6 0.1 reshape.52
  2.7 0.7 broadcast_in_dim.39.held
  3.3 1.5 select_reduce_fusion
  4.8 0.7 subtract_select_fusion
  5.5 1.6 lt.34
  7.1 1.9 copy.14
  9.1 0.1 lt.32
  9.2 1.2 select_convert_fusion.bias
  10.4 231.9 %shard_map.104 = (bf16[512,1024]{1,0:T(8,128)(2,1)}, bf16[512,1024]{1,0:T(8,128)(2,1)}) custom-call(s32[4]{0:T(128)} %get-tuple-element.3.slot_core, s32[4]{0:T(128)} %get-tuple-element.2.slot_index, f32[8,128]{1,0:T(8,128)} %broadcast_in_dim.39.held, bf16[512,1024]{1,0:T(8,128)(2,1)} %tok.1, bf16[512,1024]{1,0:T(8,128)(2,1)} %dec.1, bf16[8192,1024]{1,0:T(8,128)(2,1)} %wq.1, ...), custom_call_target="tpu_custom_call" | custom-call | flops 21474836480 | bytes 31457280 | tf_op jit(solution)/shard_map/pallas_call | solution.py:508
  242.3 2.3 copy.17
  244.6 2.3 copy.18
  (3 shorter events, 0.0 us)
Async XLA Ops:
  0.6 0.7 copy-start
